TPU v7x, 256 devices: a whole 4x4x8 slice. The times are simulated.
256 devices in a mesh: dom: 32 (over z, y), feat: 8 (over x, core).
Axes of the slice: x: 4, y: 4, z: 8, core: 2. Of those that a mesh axis runs over, the one named last changes fastest.
Arguments:
- features: bfloat16 [8192, 8, 25088], P('dom', 'feat'), may hold values from -50 to 50, as said below
- weights: float32 [8, 32, 25088], P('feat', None, 'dom'), may hold values from -6 to 6
- geno_live: int32 [4], replicated, may hold values from 1 to 25088, 100000 in all
- image_live: int32 [4], replicated, may hold values from 1 to 12544, 50000 in all
Outputs:
- updated: float32 [8, 32, 25088], P('feat', None, 'dom')
Inputs may be any that keep to these rules, and one draw needn't show every extreme that they name: `features`: rows are participants; every entry is finite. `geno_live`: the counts sum to 100000. `image_live`: the counts sum to 50000.
All inputs are finite; a program needn't handle non-finite values.
Results may differ from a plain program's by a relative error of at most 0.0048.
Values may be sent and summed in bfloat16 or wider, within the bound.
No kernel may reach another device: no remote copies, remote signals or barrier semaphores. Data moves between devices by JAX's collectives and lax.ppermute only.
A program may use at most 64 MiB of HBM per device.

v0:
```python
import functools
import jax
import jax.numpy as jnp
from jax import lax
from jax.experimental import pallas as pl
from jax.experimental.pallas import tpu as pltpu
from jax.sharding import Mesh
from jax.sharding import PartitionSpec as P

GX = 100000
GY = 50000
K = 32
ITERS = 2
LANES = 128
STEPS = ((1, 0), (0, 1), (1, 1))
HERE = (0, 0)
FAR = ("za", "ya")
DOM = ("za", "zb", "ya", "yb")
AXES = DOM + ("feat",)
CHUNKS = 8
GROUP = 8
step_rate = 0.1
jitter = 1e-05

VMEM = pl.BlockSpec(memory_space=pltpu.VMEM)
SMEM = pl.BlockSpec(memory_space=pltpu.SMEM)
SMALL = 24 * 1024 * 1024
MEDIUM = 36 * 1024 * 1024
LARGE = 60 * 1024 * 1024
HIGH = lax.Precision.HIGHEST
F32 = jnp.float32
BF16 = jnp.bfloat16


def padded(width):
    return -(-width // LANES) * LANES


def window(width):
    return padded(width + LANES - 16)


def base_of(index, width):
    return (index * width) // LANES * LANES


def offset_of(index, width):
    return lax.rem(index * width, LANES)


def moved(values, source, target, width):
    size = values.shape[1]
    lane = lax.broadcasted_iota(jnp.int32, values.shape, 1)
    values = jnp.where((lane >= source) & (lane < source + width), values, 0.0)
    return pltpu.roll(values, lax.rem(target - source + size, size), 1)


def far_index():
    return lax.axis_index("za") * lax.axis_size("ya") + lax.axis_index("ya")


def shard_index(part, step):
    ya = lax.axis_size("ya")
    z = part // ya * 2 + lax.rem(lax.axis_index("zb") + step[0], 2)
    y = part % ya * 2 + lax.rem(lax.axis_index("yb") + step[1], 2)
    return z * (2 * ya) + y


def route(step, zs, ys, feats):
    def partner(place, size, odd, flip):
        return (place + (1 if place % 2 == odd else -1)) % size if flip else place

    pairs = []
    for z in range(zs):
        for y in range(ys):
            for feat in range(feats):
                odd = feat % 2
                to_z = partner(z, zs, odd, step[0])
                to_y = partner(y, ys, odd, step[1])
                pairs.append(((z * ys + y) * feats + feat, (to_z * ys + to_y) * feats + feat))
    return pairs


def send(message, step):
    zs, ys = 2 * lax.axis_size("za"), 2 * lax.axis_size("ya")
    return lax.ppermute(message, AXES, route(step, zs, ys, lax.axis_size("feat")))


def columns_of(part, step, width):
    begin = shard_index(part, step) * width
    base = pl.multiple_of(lax.div(begin, LANES) * LANES, LANES)
    return pl.ds(base, window(width)), lax.rem(begin, LANES)


def is_geno():
    return lax.axis_index("feat") < lax.axis_size("feat") // 2


def lane_mask(geno_live, image_live, width):
    slot = lax.rem(lax.axis_index("feat"), lax.axis_size("feat") // 2)
    live = jnp.where(is_geno(), geno_live[slot], image_live[slot])
    shard = lax.axis_index(DOM)
    column = lax.broadcasted_iota(jnp.int32, (K, width), 1) + shard * width
    return (column < live).astype(F32)


def spread(masked, width, pad, copies):
    pad[...] = jnp.zeros(pad.shape, F32)
    pad[:, :width] = masked
    shift = offset_of(far_index(), width)
    rounded = pltpu.roll(pad[...], shift, 1).astype(BF16)
    for copy in range(copies.shape[0]):
        copies[copy] = rounded


def first_kernel(geno_live, image_live, weights, copies, pad):
    width = weights.shape[1]
    masked = weights[...] * lane_mask(geno_live, image_live, width)
    spread(masked, width, pad, copies)


def join_kernel(width, windows, joined):
    size = windows.shape[2]
    joined[...] = jnp.zeros(joined.shape, BF16)
    for part in range(windows.shape[0]):
        base = base_of(part, width)
        joined[:, base : base + size] += windows[part]


def projected(far, steps, pieces, features, total):
    width = features.shape[1] // (far * 4)
    size = window(width)
    for step, piece in zip(steps, pieces):
        for part in range(far):
            columns, begin = columns_of(part, step, width)
            start = base_of(part, width)
            weights = piece[:, start : start + size].astype(F32)
            weights = moved(weights, part * width % LANES, begin, width).astype(BF16)
            product = lax.dot_general(
                features[:, columns],
                weights,
                (((1,), (1,)), ((), ())),
                preferred_element_type=F32,
            )
            total = product if total is None else total + product
    return total


def project_first_kernel(far, features, joined, total, held, arrived):
    rows = features.shape[0] // CHUNKS
    copies = []
    for chunk in range(CHUNKS):
        place = pl.ds(chunk * rows, rows)
        copies.append(
            pltpu.make_async_copy(features.at[place], held.at[place], arrived.at[chunk])
        )
        copies[-1].start()
    for copy in copies:
        copy.wait()
    total[...] = projected(far, (HERE,), (joined,), held, None)


def project_own_kernel(far, steps, features, *rest):
    *pieces, total = rest
    total[...] = projected(far, steps, pieces, features, None)


def project_kernel(far, steps, features, before, *rest):
    *pieces, total = rest
    total[...] = projected(far, steps, pieces, features, before[...])


def project_last_kernel(far, steps, features, before, *rest):
    *pieces, copies = rest
    total = projected(far, steps, pieces, features, before[...]).T
    for copy in range(copies.shape[0]):
        copies[copy] = total


def gram_kernel(partials, own, partner, copies):
    half = partials.shape[0] // 2
    geno = partials[0]
    image = partials[half]
    for block in range(1, half):
        geno += partials[block]
        image += partials[half + block]
    geno *= GX ** (-0.5)
    image *= GY ** (-0.5)
    own[...] = jnp.where(is_geno(), geno, image)
    other = jnp.where(is_geno(), image, geno)
    partner[...] = other
    tiled = jnp.concatenate([other] * (LANES // K), axis=0)
    gram = lax.dot_general(
        other, tiled, (((1,), (1,)), ((), ())), precision=HIGH, preferred_element_type=F32
    )
    lane = lax.broadcasted_iota(jnp.int32, (8, LANES), 1)
    packed = jnp.zeros((8, LANES), F32)
    for part in range(LANES // K):
        packed = jnp.where(lane // K == part, gram[8 * part : 8 * part + 8], packed)
    for copy in range(copies.shape[0]):
        copies[copy] = packed


def message_row(far, step, residual, features, row):
    width = features.shape[1] // (far * 4)
    size = window(width)
    row[...] = jnp.zeros(row.shape, F32)
    for part in range(far):
        columns, begin = columns_of(part, step, width)
        piece = lax.dot_general(
            residual[...],
            features[:, columns],
            (((1,), (0,)), ((), ())),
            preferred_element_type=F32,
        )
        start = base_of(part, width)
        row[:, start : start + size] += moved(piece, begin, part * width % LANES, width)


def residual_kernel(participants, far, grams, own, partner, features, residual, message, row_sum):
    total = grams[0]
    for part in range(1, grams.shape[0]):
        total += grams[part]
    rows = [total] + [pltpu.roll(total, LANES - K * part, 1) for part in range(1, LANES // K)]
    row = lax.broadcasted_iota(jnp.int32, (K, LANES), 0)
    lane = lax.broadcasted_iota(jnp.int32, (K, LANES), 1)
    covariance = jnp.concatenate(rows, axis=0) / participants
    covariance += jnp.where(lane == row, jitter, 0.0)
    state = jnp.where(lane < K, covariance, jnp.where(lane == row + K, 1.0, 0.0))
    for base in range(0, K, GROUP):
        columns = [
            jnp.broadcast_to(state[:, base + i : base + i + 1], state.shape) for i in range(GROUP)
        ]
        rows = [state[base + i : base + i + 1, :] for i in range(GROUP)]
        for i in range(GROUP):
            step = base + i
            inverse = 1.0 / columns[i][step : step + 1, :]
            below = jnp.where(row > step, columns[i], 0.0)
            for later in range(i + 1, GROUP):
                ratio = columns[i][base + later : base + later + 1, :] * inverse
                columns[later] = columns[later] - below * ratio
                rows[later] = rows[later] - rows[i] * ratio
            state = state - below * (rows[i] * inverse)
    pivots = jnp.sum(jnp.where(lane == row, state, 0.0), axis=1, keepdims=True)
    scaled = state * lax.rsqrt(pivots)
    inverse = pltpu.roll(scaled, LANES - K, 1)[:, :K]
    target = lax.dot_general(
        inverse, partner[...], (((1,), (0,)), ((), ())), precision=HIGH, preferred_element_type=F32
    )
    residual[...] = (own[...] - target).astype(BF16)
    message_row(far, STEPS[2], residual, features, row_sum)
    message[...] = row_sum[...].astype(BF16)


def message_kernel(far, steps, residual, features, *rest):
    *messages, row = rest
    for step, message in zip(steps, messages):
        message_row(far, step, residual, features, row)
        message[...] = row[...].astype(BF16)


def kept_kernel(far, residual, features, received, kept):
    message_row(far, HERE, residual, features, kept)
    kept[...] += received[...].astype(F32)


def fold_kernel(width, own, *rest):
    *received, windows = rest
    total = own[...]
    for message in received:
        total += message[...].astype(F32)
    total = total.astype(BF16)
    size = windows.shape[2]
    for part in range(windows.shape[0]):
        start = base_of(part, width)
        windows[part] = total[:, start : start + size]


def updated_weights(step_size, geno_live, image_live, windows, weights):
    width = weights.shape[1]
    total = windows[0].astype(F32)
    for part in range(1, windows.shape[0]):
        total += windows[part].astype(F32)
    size = windows.shape[2]
    shift = lax.rem(size - offset_of(far_index(), width), size)
    gradient = pltpu.roll(total, shift, 1)[:, :width]
    return lane_mask(geno_live, image_live, width) * (weights[...] - step_size * gradient)


def update_kernel(step_size, geno_live, image_live, windows, weights, updated, copies, pad):
    fresh = updated_weights(step_size, geno_live, image_live, windows, weights)
    updated[...] = fresh
    spread(fresh, weights.shape[1], pad, copies)


def last_kernel(step_size, geno_live, image_live, windows, weights, updated):
    updated[...] = updated_weights(step_size, geno_live, image_live, windows, weights)


def call(kernel, outs, scratch, specs, *operands, grant=SMALL, flops=0):
    shapes = tuple(jax.ShapeDtypeStruct(*out) for out in outs)
    return pl.pallas_call(
        kernel,
        out_shape=shapes,
        in_specs=specs,
        out_specs=tuple(VMEM for _ in shapes),
        scratch_shapes=list(scratch),
        compiler_params=pltpu.CompilerParams(vmem_limit_bytes=grant),
        cost_estimate=pl.CostEstimate(flops=flops, bytes_accessed=1 << 10, transcendentals=0),
    )(*operands)


def exchange(copies, axis):
    return lax.all_to_all(copies, axis, 0, 0, tiled=True)


def body(features, weights, geno_live, image_live):
    row_count = features.shape[0]
    own_block = features[:, 0, :]
    current = weights[0]
    width = current.shape[1]
    size = window(width)
    doms = lax.axis_size(DOM)
    far = lax.axis_size(FAR)
    feats = lax.axis_size("feat")
    participants = row_count * doms
    step_size = step_rate * participants ** (-0.5)

    joined_size = base_of(far - 1, width) + size
    pad = pltpu.VMEM((K, size), F32)
    line = ((far, K, size), BF16)
    message = ((K, joined_size), BF16)
    rows = ((K, row_count), F32)
    total = ((row_count, K), F32)
    partial = ((feats, K, row_count), F32)
    piece_flops = 2 * row_count * K * joined_size

    def project(kernel, out, steps, *operands):
        kernel = functools.partial(kernel, far, steps)
        flops = piece_flops * len(steps)
        return call(kernel, [out], [], [VMEM] * len(operands), *operands, flops=flops)[0]

    def messages(residual, held, steps):
        return call(
            functools.partial(message_kernel, far, steps),
            [message] * len(steps),
            [pltpu.VMEM(message[0], F32)],
            [VMEM, VMEM],
            residual,
            held,
            flops=piece_flops * len(steps) * 8,
        )

    (copies,) = call(
        first_kernel,
        [line],
        [pad],
        [SMEM, SMEM, VMEM],
        geno_live,
        image_live,
        current,
        grant=LARGE,
    )
    for sweep in range(ITERS):
        windows = exchange(copies, FAR)
        (joined,) = call(
            functools.partial(join_kernel, width), [message], [], [VMEM], windows
        )
        received = [send(joined, step) for step in STEPS]
        if sweep == 0:
            part, held = call(
                functools.partial(project_first_kernel, far),
                [total, (own_block.shape, BF16)],
                [pltpu.SemaphoreType.DMA((CHUNKS,))],
                [pl.BlockSpec(memory_space=pl.ANY), VMEM],
                own_block,
                joined,
                grant=MEDIUM,
                flops=piece_flops,
            )
        else:
            part = project(project_own_kernel, total, (HERE,), held, joined)
        part = project(project_kernel, total, STEPS[:2], held, part, *received[:2])
        copies = project(project_last_kernel, partial, STEPS[2:], held, part, *received[2:])
        partials = exchange(copies, "feat")
        own, partner, copies = call(
            gram_kernel, [rows, rows, ((doms, 8, LANES), F32)], [], [VMEM], partials
        )
        grams = exchange(copies, DOM)
        residual, made = call(
            functools.partial(residual_kernel, participants, far),
            [((K, row_count), BF16), message],
            [pltpu.VMEM(message[0], F32)],
            [VMEM] * 4,
            grams,
            own,
            partner,
            held,
        )
        first = send(made, STEPS[2])
        made = messages(residual, held, STEPS[:2])
        received = [send(item, step) for item, step in zip(made, STEPS[:2])]
        kernel = functools.partial(kept_kernel, far)
        (kept,) = call(
            kernel, [(message[0], F32)], [], [VMEM] * 3, residual, held, first, flops=piece_flops * 8
        )
        kernel = functools.partial(fold_kernel, width)
        (copies,) = call(kernel, [line], [], [VMEM] * 3, kept, *received)
        shares = exchange(copies, FAR)
        operands = (geno_live, image_live, shares, current)
        specs = [SMEM, SMEM, VMEM, VMEM]
        if sweep < ITERS - 1:
            kernel = functools.partial(update_kernel, step_size)
            current, copies = call(kernel, [(current.shape, F32), line], [pad], specs, *operands)
        else:
            kernel = functools.partial(last_kernel, step_size)
            (current,) = call(kernel, [(current.shape, F32)], [], specs, *operands)
    return current[None]


def solution(mesh):
    ys = 4
    shape = (mesh.shape["dom"] // ys // 2, 2, ys // 2, 2, mesh.shape["feat"])
    split = Mesh(mesh.devices.reshape(shape), AXES)
    placed = (P(DOM, "feat", None), P("feat", None, DOM), P(), P())
    return jax.shard_map(
        body, mesh=split, in_specs=placed, out_specs=P("feat", None, DOM), check_vma=False
    )
```

profile of v0, /device:TPU:8, one launch (start us, length us, event | category | flops | bytes accessed | tf_op | source)
XLA Modules:
  0.0 199.0 jit_solution(14282130397456018513)
XLA Ops:
  0.0 1.8 shard_map.46
  1.8 25.8 %all_to_all.40.windows = bf16[8,32,896]{2,1,0:T(8,128)(2,1)S(1)} all-to-all(bf16[8,32,896]{2,1,0:T(8,128)(2,1)} %shard_map.46), channel_id=1, replica_groups=mesh['za'=4,'zb'=2,'ya'=2,'yb'=2,'feat'=8] {'za','ya'}, dimensions={0} | all-to-all | bytes 917504 | tf_op jit(solution)/shard_map/all_to_all | solution.py:314
  29.1 2.0 %collective-permute-start = (bf16[32,6272]{1,0:T(8,128)(2,1)S(1)}, bf16[32,6272]{1,0:T(8,128)(2,1)S(1)}, u32[]{:S(2)}, u32[]{:S(2)}) collective-permute-start(bf16[32,6272]{1,0:T(8,128)(2,1)S(1)} %shard_map.47.joined), channel_id=1, source_target_pairs={{0,32},{1,225},{2,34},{3,227},{4,36},{5,229},{6,38},{7,231},{8,40}... | collective-permute-start | bytes 1204232 | tf_op jit(solution)/shard_map/ppermute | solution.py:86
  31.3 6.0 %shard_map.48 = (f32[256,32]{1,0:T(8,128)S(1)}, bf16[256,25088]{1,0:T(8,128)(2,1)S(1)}) custom-call(bf16[256,25088]{1,0:T(8,128)(2,1)} %bitcast.5, bf16[32,6272]{1,0:T(8,128)(2,1)S(1)} %shard_map.47.joined), custom_call_target="tpu_custom_call" | custom-call | flops 102760448 | bytes 1024 | tf_op jit(solution)/shard_map/pallas_call | solution.py:302
  37.3 2.2 %shard_map.49.before = f32[256,32]{1,0:T(8,128)S(1)} custom-call(bf16[256,25088]{1,0:T(8,128)(2,1)S(1)} %get-tuple-element.23.features, f32[256,32]{1,0:T(8,128)S(1)} %get-tuple-element.24.before, bf16[32,6272]{1,0:T(8,128)(2,1)S(1)} %collective-permute-done.rest_0_, bf16[32,6272]{1,0:T(8,128)(2,1)S(1)} %collective-permute-done.1.rest_1_), custom_call_target="tpu_custom_call" | custom-call | flops 205520896 | bytes 1024 | tf_op jit(solution)/shard_map/pallas_call | solution.py:302
  39.5 1.9 collective-permute-done.2.rest_0_
  42.7 11.6 %all_to_all.41.partials = f32[8,32,256]{2,1,0:T(8,128)S(1)} all-to-all(f32[8,32,256]{2,1,0:T(8,128)S(1)} %shard_map.50), channel_id=1, replica_groups=mesh['za'=4,'zb'=2,'ya'=2,'yb'=2,'feat'=8] {'feat'}, dimensions={0} | all-to-all | bytes 524288 | tf_op jit(solution)/shard_map/all_to_all | solution.py:314
  54.6 15.0 %all_to_all.42.grams = f32[32,8,128]{2,1,0:T(8,128)S(1)} all-to-all(f32[32,8,128]{2,1,0:T(8,128)S(1)} %get-tuple-element.25), channel_id=1, replica_groups=mesh['za'=4,'zb'=2,'ya'=2,'yb'=2,'feat'=8] {'za','zb','ya','yb'}, dimensions={0} | all-to-all | bytes 262144 | tf_op jit(solution)/shard_map/all_to_all | solution.py:314
  71.3 2.2 %collective-permute-start.3 = (bf16[32,6272]{1,0:T(8,128)(2,1)S(1)}, bf16[32,6272]{1,0:T(8,128)(2,1)S(1)}, u32[]{:S(2)}, u32[]{:S(2)}) collective-permute-start(bf16[32,6272]{1,0:T(8,128)(2,1)S(1)} %get-tuple-element.29), channel_id=1, source_target_pairs={{0,40},{1,249},{2,42},{3,251},{4,44},{5,253},{6,46},{7,255},{8,32}... | collective-permute-start | bytes 1204232 | tf_op jit(solution)/shard_map/ppermute | solution.py:86
  76.3 4.0 %collective-permute-done.3.received = bf16[32,6272]{1,0:T(8,128)(2,1)S(1)} collective-permute-done((bf16[32,6272]{1,0:T(8,128)(2,1)S(1)}, bf16[32,6272]{1,0:T(8,128)(2,1)S(1)}, u32[]{:S(2)}, u32[]{:S(2)}) %collective-permute-start.3) | collective-permute-done | bytes 401440 | tf_op jit(solution)/shard_map/ppermute | solution.py:86
  81.0 4.0 %collective-permute-done.4.rest_0_ = bf16[32,6272]{1,0:T(8,128)(2,1)S(1)} collective-permute-done((bf16[32,6272]{1,0:T(8,128)(2,1)S(1)}, bf16[32,6272]{1,0:T(8,128)(2,1)S(1)}, u32[]{:S(2)}, u32[]{:S(2)}) %collective-permute-start.4) | collective-permute-done | bytes 401440 | tf_op jit(solution)/shard_map/ppermute | solution.py:86
  85.1 18.9 %all_to_all.43.windows = bf16[8,32,896]{2,1,0:T(8,128)(2,1)S(1)} all-to-all(bf16[8,32,896]{2,1,0:T(8,128)(2,1)S(1)} %shard_map.55), channel_id=1, replica_groups=mesh['za'=4,'zb'=2,'ya'=2,'yb'=2,'feat'=8] {'za','ya'}, dimensions={0} | all-to-all | bytes 917504 | tf_op jit(solution)/shard_map/all_to_all | solution.py:314
  104.9 19.1 %all_to_all.44.windows = bf16[8,32,896]{2,1,0:T(8,128)(2,1)S(1)} all-to-all(bf16[8,32,896]{2,1,0:T(8,128)(2,1)S(1)} %get-tuple-element.32), channel_id=1, replica_groups=mesh['za'=4,'zb'=2,'ya'=2,'yb'=2,'feat'=8] {'za','ya'}, dimensions={0} | all-to-all | bytes 917504 | tf_op jit(solution)/shard_map/all_to_all | solution.py:314
  124.6 1.8 collective-permute-start.6
  129.0 3.1 %collective-permute-done.7.rest_1_ = bf16[32,6272]{1,0:T(8,128)(2,1)S(1)} collective-permute-done((bf16[32,6272]{1,0:T(8,128)(2,1)S(1)}, bf16[32,6272]{1,0:T(8,128)(2,1)S(1)}, u32[]{:S(2)}, u32[]{:S(2)}) %collective-permute-start.7) | collective-permute-done | bytes 401440 | tf_op jit(solution)/shard_map/ppermute | solution.py:86
  132.5 2.2 %shard_map.59.before = f32[256,32]{1,0:T(8,128)S(1)} custom-call(bf16[256,25088]{1,0:T(8,128)(2,1)S(1)} %get-tuple-element.23.features, f32[256,32]{1,0:T(8,128)S(1)} %shard_map.58.before, bf16[32,6272]{1,0:T(8,128)(2,1)S(1)} %collective-permute-done.6.rest_0_, bf16[32,6272]{1,0:T(8,128)(2,1)S(1)} %collective-permute-done.7.rest_1_), custom_call_target="tpu_custom_call" | custom-call | flops 205520896 | bytes 1024 | tf_op jit(solution)/shard_map/pallas_call | solution.py:302
  134.7 3.2 %collective-permute-done.8.rest_0_ = bf16[32,6272]{1,0:T(8,128)(2,1)S(1)} collective-permute-done((bf16[32,6272]{1,0:T(8,128)(2,1)S(1)}, bf16[32,6272]{1,0:T(8,128)(2,1)S(1)}, u32[]{:S(2)}, u32[]{:S(2)}) %collective-permute-start.8) | collective-permute-done | bytes 401440 | tf_op jit(solution)/shard_map/ppermute | solution.py:86
  139.2 9.9 %all_to_all.45.partials = f32[8,32,256]{2,1,0:T(8,128)S(1)} all-to-all(f32[8,32,256]{2,1,0:T(8,128)S(1)} %shard_map.60), channel_id=1, replica_groups=mesh['za'=4,'zb'=2,'ya'=2,'yb'=2,'feat'=8] {'feat'}, dimensions={0} | all-to-all | bytes 524288 | tf_op jit(solution)/shard_map/all_to_all | solution.py:314
  149.4 13.9 %all_to_all.46.grams = f32[32,8,128]{2,1,0:T(8,128)S(1)} all-to-all(f32[32,8,128]{2,1,0:T(8,128)S(1)} %get-tuple-element.33), channel_id=1, replica_groups=mesh['za'=4,'zb'=2,'ya'=2,'yb'=2,'feat'=8] {'za','zb','ya','yb'}, dimensions={0} | all-to-all | bytes 262144 | tf_op jit(solution)/shard_map/all_to_all | solution.py:314
  163.3 1.7 shard_map.62
  165.0 2.2 %collective-permute-start.9 = (bf16[32,6272]{1,0:T(8,128)(2,1)S(1)}, bf16[32,6272]{1,0:T(8,128)(2,1)S(1)}, u32[]{:S(2)}, u32[]{:S(2)}) collective-permute-start(bf16[32,6272]{1,0:T(8,128)(2,1)S(1)} %get-tuple-element.37), channel_id=1, source_target_pairs={{0,40},{1,249},{2,42},{3,251},{4,44},{5,253},{6,46},{7,255},{8,32}... | collective-permute-start | bytes 1204232 | tf_op jit(solution)/shard_map/ppermute | solution.py:86
  169.9 4.0 %collective-permute-done.9.received = bf16[32,6272]{1,0:T(8,128)(2,1)S(1)} collective-permute-done((bf16[32,6272]{1,0:T(8,128)(2,1)S(1)}, bf16[32,6272]{1,0:T(8,128)(2,1)S(1)}, u32[]{:S(2)}, u32[]{:S(2)}) %collective-permute-start.9) | collective-permute-done | bytes 401440 | tf_op jit(solution)/shard_map/ppermute | solution.py:86
  174.6 4.0 %collective-permute-done.10.rest_0_ = bf16[32,6272]{1,0:T(8,128)(2,1)S(1)} collective-permute-done((bf16[32,6272]{1,0:T(8,128)(2,1)S(1)}, bf16[32,6272]{1,0:T(8,128)(2,1)S(1)}, u32[]{:S(2)}, u32[]{:S(2)}) %collective-permute-start.10) | collective-permute-done | bytes 401440 | tf_op jit(solution)/shard_map/ppermute | solution.py:86
  178.8 18.9 %all_to_all.47.windows = bf16[8,32,896]{2,1,0:T(8,128)(2,1)S(1)} all-to-all(bf16[8,32,896]{2,1,0:T(8,128)(2,1)S(1)} %shard_map.65), channel_id=1, replica_groups=mesh['za'=4,'zb'=2,'ya'=2,'yb'=2,'feat'=8] {'za','ya'}, dimensions={0} | all-to-all | bytes 917504 | tf_op jit(solution)/shard_map/all_to_all | solution.py:314
  (35 shorter events, 19.3 us)
Async XLA Ops:
  27.7 9.6 %collective-permute-start.1 = (bf16[32,6272]{1,0:T(8,128)(2,1)S(1)}, bf16[32,6272]{1,0:T(8,128)(2,1)S(1)}, u32[]{:S(2)}, u32[]{:S(2)}) collective-permute-start(bf16[32,6272]{1,0:T(8,128)(2,1)S(1)} %shard_map.47.joined), channel_id=1, source_target_pairs={{0,8},{1,25},{2,10},{3,27},{4,12},{5,29},{6,14},{7,31},{8,0},{9,17... | collective-permute-start | bytes 1204232 | tf_op jit(solution)/shard_map/ppermute | solution.py:86
  29.1 8.2 %collective-permute-start = (bf16[32,6272]{1,0:T(8,128)(2,1)S(1)}, bf16[32,6272]{1,0:T(8,128)(2,1)S(1)}, u32[]{:S(2)}, u32[]{:S(2)}) collective-permute-start(bf16[32,6272]{1,0:T(8,128)(2,1)S(1)} %shard_map.47.joined), channel_id=1, source_target_pairs={{0,32},{1,225},{2,34},{3,227},{4,36},{5,229},{6,38},{7,231},{8,40}... | collective-permute-start | bytes 1204232 | tf_op jit(solution)/shard_map/ppermute | solution.py:86
  31.1 10.3 %collective-permute-start.2 = (bf16[32,6272]{1,0:T(8,128)(2,1)S(1)}, bf16[32,6272]{1,0:T(8,128)(2,1)S(1)}, u32[]{:S(2)}, u32[]{:S(2)}) collective-permute-start(bf16[32,6272]{1,0:T(8,128)(2,1)S(1)} %shard_map.47.joined), channel_id=1, source_target_pairs={{0,40},{1,249},{2,42},{3,251},{4,44},{5,253},{6,46},{7,255},{8,32}... | collective-permute-start | bytes 1204232 | tf_op jit(solution)/shard_map/ppermute | solution.py:86
  71.3 8.9 %collective-permute-start.3 = (bf16[32,6272]{1,0:T(8,128)(2,1)S(1)}, bf16[32,6272]{1,0:T(8,128)(2,1)S(1)}, u32[]{:S(2)}, u32[]{:S(2)}) collective-permute-start(bf16[32,6272]{1,0:T(8,128)(2,1)S(1)} %get-tuple-element.29), channel_id=1, source_target_pairs={{0,40},{1,249},{2,42},{3,251},{4,44},{5,253},{6,46},{7,255},{8,32}... | collective-permute-start | bytes 1204232 | tf_op jit(solution)/shard_map/ppermute | solution.py:86
  73.6 30.5 %copy-start = (f32[1,32,784]{2,1,0:T(8,128)S(1)}, f32[1,32,784]{2,1,0:T(8,128)}, u32[]{:S(2)}) copy-start(f32[1,32,784]{2,1,0:T(8,128)} %param.5) | copy-start | bytes 301060
  73.6 30.5 %copy-start.1 = (s32[4]{0:T(128)S(1)}, s32[4]{0:T(128)}, u32[]{:S(2)}) copy-start(s32[4]{0:T(128)} %geno_live.5) | copy-start | bytes 52
  73.6 30.5 %copy-start.2 = (s32[4]{0:T(128)S(1)}, s32[4]{0:T(128)}, u32[]{:S(2)}) copy-start(s32[4]{0:T(128)} %image_live.5) | copy-start | bytes 52
  74.8 10.1 %collective-permute-start.4 = (bf16[32,6272]{1,0:T(8,128)(2,1)S(1)}, bf16[32,6272]{1,0:T(8,128)(2,1)S(1)}, u32[]{:S(2)}, u32[]{:S(2)}) collective-permute-start(bf16[32,6272]{1,0:T(8,128)(2,1)S(1)} %get-tuple-element.30), channel_id=1, source_target_pairs={{0,32},{1,225},{2,34},{3,227},{4,36},{5,229},{6,38},{7,231},{8,40}... | collective-permute-start | bytes 1204232 | tf_op jit(solution)/shard_map/ppermute | solution.py:86
  76.1 8.8 %collective-permute-start.5 = (bf16[32,6272]{1,0:T(8,128)(2,1)S(1)}, bf16[32,6272]{1,0:T(8,128)(2,1)S(1)}, u32[]{:S(2)}, u32[]{:S(2)}) collective-permute-start(bf16[32,6272]{1,0:T(8,128)(2,1)S(1)} %get-tuple-element.31), channel_id=1, source_target_pairs={{0,8},{1,25},{2,10},{3,27},{4,12},{5,29},{6,14},{7,31},{8,0},{9,17... | collective-permute-start | bytes 1204232 | tf_op jit(solution)/shard_map/ppermute | solution.py:86
  124.0 8.1 %collective-permute-start.7 = (bf16[32,6272]{1,0:T(8,128)(2,1)S(1)}, bf16[32,6272]{1,0:T(8,128)(2,1)S(1)}, u32[]{:S(2)}, u32[]{:S(2)}) collective-permute-start(bf16[32,6272]{1,0:T(8,128)(2,1)S(1)} %shard_map.57.rest_0_), channel_id=1, source_target_pairs={{0,8},{1,25},{2,10},{3,27},{4,12},{5,29},{6,14},{7,31},{8,0},{9,17... | collective-permute-start | bytes 1204232 | tf_op jit(solution)/shard_map/ppermute | solution.py:86
  124.6 7.9 %collective-permute-start.6 = (bf16[32,6272]{1,0:T(8,128)(2,1)S(1)}, bf16[32,6272]{1,0:T(8,128)(2,1)S(1)}, u32[]{:S(2)}, u32[]{:S(2)}) collective-permute-start(bf16[32,6272]{1,0:T(8,128)(2,1)S(1)} %shard_map.57.rest_0_), channel_id=1, source_target_pairs={{0,32},{1,225},{2,34},{3,227},{4,36},{5,229},{6,38},{7,231},{8,40}... | collective-permute-start | bytes 1204232 | tf_op jit(solution)/shard_map/ppermute | solution.py:86
  126.4 11.5 %collective-permute-start.8 = (bf16[32,6272]{1,0:T(8,128)(2,1)S(1)}, bf16[32,6272]{1,0:T(8,128)(2,1)S(1)}, u32[]{:S(2)}, u32[]{:S(2)}) collective-permute-start(bf16[32,6272]{1,0:T(8,128)(2,1)S(1)} %shard_map.57.rest_0_), channel_id=1, source_target_pairs={{0,40},{1,249},{2,42},{3,251},{4,44},{5,253},{6,46},{7,255},{8,32}... | collective-permute-start | bytes 1204232 | tf_op jit(solution)/shard_map/ppermute | solution.py:86
  165.0 8.9 %collective-permute-start.9 = (bf16[32,6272]{1,0:T(8,128)(2,1)S(1)}, bf16[32,6272]{1,0:T(8,128)(2,1)S(1)}, u32[]{:S(2)}, u32[]{:S(2)}) collective-permute-start(bf16[32,6272]{1,0:T(8,128)(2,1)S(1)} %get-tuple-element.37), channel_id=1, source_target_pairs={{0,40},{1,249},{2,42},{3,251},{4,44},{5,253},{6,46},{7,255},{8,32}... | collective-permute-start | bytes 1204232 | tf_op jit(solution)/shard_map/ppermute | solution.py:86
  168.5 10.1 %collective-permute-start.10 = (bf16[32,6272]{1,0:T(8,128)(2,1)S(1)}, bf16[32,6272]{1,0:T(8,128)(2,1)S(1)}, u32[]{:S(2)}, u32[]{:S(2)}) collective-permute-start(bf16[32,6272]{1,0:T(8,128)(2,1)S(1)} %get-tuple-element.38), channel_id=1, source_target_pairs={{0,32},{1,225},{2,34},{3,227},{4,36},{5,229},{6,38},{7,231},{8,40}... | collective-permute-start | bytes 1204232 | tf_op jit(solution)/shard_map/ppermute | solution.py:86
  169.8 8.8 %collective-permute-start.11 = (bf16[32,6272]{1,0:T(8,128)(2,1)S(1)}, bf16[32,6272]{1,0:T(8,128)(2,1)S(1)}, u32[]{:S(2)}, u32[]{:S(2)}) collective-permute-start(bf16[32,6272]{1,0:T(8,128)(2,1)S(1)} %get-tuple-element.39), channel_id=1, source_target_pairs={{0,8},{1,25},{2,10},{3,27},{4,12},{5,29},{6,14},{7,31},{8,0},{9,17... | collective-permute-start | bytes 1204232 | tf_op jit(solution)/shard_map/ppermute | solution.py:86
where the time goes:
time: 199 us
  blocking collectives  133 us (67%)
  Pallas kernels  26.5 us (13%)
  waiting for transfers between devices  24.5 us (12%)
  starting transfers between devices  14.7 us (7%)
    all_to_all x8, blocking collectives, exchange(): return lax.all_to_all(copies, axis, 0, 0, tiled=True)  133 us
    pallas_call x21, Pallas kernels, call(): pl.pallas_call(kernel, out_shape=shapes, in_specs=specs, out_specs=tuple(...  26.5 us
    ppermute x12, waiting for transfers between devices, send(): lax.ppermute(message, AXES, route(step, zs, ys, lax.axis_size('feat')))  24.5 us
    ppermute x12, starting transfers between devices, send(): lax.ppermute(message, AXES, route(step, zs, ys, lax.axis_size('feat')))  14.7 us
  transfers between devices with their start and end apart: 12, of which 8 were waited for; matrix products, arithmetic and copies ran while one was open for 0% of the time, Pallas kernels for 8%

commit v1 on v0

--- a/solution.py
+++ b/solution.py
@@ -113,10 +113,10 @@
         copies[copy] = rounded
 
 
-def first_kernel(geno_live, image_live, weights, copies, pad):
+def first_kernel(geno_live, image_live, weights, copies, mask, pad):
     width = weights.shape[1]
-    masked = weights[...] * lane_mask(geno_live, image_live, width)
-    spread(masked, width, pad, copies)
+    mask[...] = lane_mask(geno_live, image_live, width)
+    spread(weights[...] * mask[...], width, pad, copies)
 
 
 def join_kernel(width, windows, joined):
@@ -276,7 +276,7 @@
         windows[part] = total[:, start : start + size]
 
 
-def updated_weights(step_size, geno_live, image_live, windows, weights):
+def updated_weights(step_size, mask, windows, weights):
     width = weights.shape[1]
     total = windows[0].astype(F32)
     for part in range(1, windows.shape[0]):
@@ -284,17 +284,17 @@
     size = windows.shape[2]
     shift = lax.rem(size - offset_of(far_index(), width), size)
     gradient = pltpu.roll(total, shift, 1)[:, :width]
-    return lane_mask(geno_live, image_live, width) * (weights[...] - step_size * gradient)
-
-
-def update_kernel(step_size, geno_live, image_live, windows, weights, updated, copies, pad):
-    fresh = updated_weights(step_size, geno_live, image_live, windows, weights)
+    return mask[...] * (weights[...] - step_size * gradient)
+
+
+def update_kernel(step_size, mask, windows, weights, updated, copies, pad):
+    fresh = updated_weights(step_size, mask, windows, weights)
     updated[...] = fresh
     spread(fresh, weights.shape[1], pad, copies)
 
 
-def last_kernel(step_size, geno_live, image_live, windows, weights, updated):
-    updated[...] = updated_weights(step_size, geno_live, image_live, windows, weights)
+def last_kernel(step_size, mask, windows, weights, updated):
+    updated[...] = updated_weights(step_size, mask, windows, weights)
 
 
 def call(kernel, outs, scratch, specs, *operands, grant=SMALL, flops=0):
@@ -351,9 +351,9 @@
             flops=piece_flops * len(steps) * 8,
         )
 
-    (copies,) = call(
+    copies, mask = call(
         first_kernel,
-        [line],
+        [line, (current.shape, F32)],
         [pad],
         [SMEM, SMEM, VMEM],
         geno_live,
@@ -407,8 +407,8 @@
         kernel = functools.partial(fold_kernel, width)
         (copies,) = call(kernel, [line], [], [VMEM] * 3, kept, *received)
         shares = exchange(copies, FAR)
-        operands = (geno_live, image_live, shares, current)
-        specs = [SMEM, SMEM, VMEM, VMEM]
+        operands = (mask, shares, current)
+        specs = [VMEM] * 3
         if sweep < ITERS - 1:
             kernel = functools.partial(update_kernel, step_size)
             current, copies = call(kernel, [(current.shape, F32), line], [pad], specs, *operands)

time: 199 us -> 198 us (level)
  no operation moved by 1% of the time
where the time goes in v1:
time: 198 us
  blocking collectives  133 us (67%)
  Pallas kernels  25.4 us (13%)
  waiting for transfers between devices  24.6 us (12%)
  starting transfers between devices  14.7 us (7%)
    all_to_all x8, blocking collectives, exchange(): return lax.all_to_all(copies, axis, 0, 0, tiled=True)  133 us
    pallas_call x21, Pallas kernels, call(): pl.pallas_call(kernel, out_shape=shapes, in_specs=specs, out_specs=tuple(...  25.4 us
    ppermute x12, waiting for transfers between devices, send(): lax.ppermute(message, AXES, route(step, zs, ys, lax.axis_size('feat')))  24.6 us
    ppermute x12, starting transfers between devices, send(): lax.ppermute(message, AXES, route(step, zs, ys, lax.axis_size('feat')))  14.7 us
  transfers between devices with their start and end apart: 12, of which 8 were waited for; matrix products, arithmetic and copies ran while one was open for 0% of the time, Pallas kernels for 8%

profile of v1, /device:TPU:8, one launch (start us, length us, event | category | flops | bytes accessed | tf_op | source)
XLA Modules:
  0.0 197.9 jit_solution(9326952249296669300)
XLA Ops:
  0.0 1.8 shard_map.46
  1.8 25.8 %all_to_all.40.windows = bf16[8,32,896]{2,1,0:T(8,128)(2,1)S(1)} all-to-all(bf16[8,32,896]{2,1,0:T(8,128)(2,1)} %get-tuple-element.26), channel_id=1, replica_groups=mesh['za'=4,'zb'=2,'ya'=2,'yb'=2,'feat'=8] {'za','ya'}, dimensions={0} | all-to-all | bytes 917504 | tf_op jit(solution)/shard_map/all_to_all | solution.py:314
  29.1 2.0 %collective-permute-start = (bf16[32,6272]{1,0:T(8,128)(2,1)S(1)}, bf16[32,6272]{1,0:T(8,128)(2,1)S(1)}, u32[]{:S(2)}, u32[]{:S(2)}) collective-permute-start(bf16[32,6272]{1,0:T(8,128)(2,1)S(1)} %shard_map.47.joined), channel_id=1, source_target_pairs={{0,32},{1,225},{2,34},{3,227},{4,36},{5,229},{6,38},{7,231},{8,40}... | collective-permute-start | bytes 1204232 | tf_op jit(solution)/shard_map/ppermute | solution.py:86
  31.3 6.0 %shard_map.48 = (f32[256,32]{1,0:T(8,128)S(1)}, bf16[256,25088]{1,0:T(8,128)(2,1)S(1)}) custom-call(bf16[256,25088]{1,0:T(8,128)(2,1)} %bitcast.5, bf16[32,6272]{1,0:T(8,128)(2,1)S(1)} %shard_map.47.joined), custom_call_target="tpu_custom_call" | custom-call | flops 102760448 | bytes 1024 | tf_op jit(solution)/shard_map/pallas_call | solution.py:302
  37.3 2.2 %shard_map.49.before = f32[256,32]{1,0:T(8,128)S(1)} custom-call(bf16[256,25088]{1,0:T(8,128)(2,1)S(1)} %get-tuple-element.27.features, f32[256,32]{1,0:T(8,128)S(1)} %get-tuple-element.28.before, bf16[32,6272]{1,0:T(8,128)(2,1)S(1)} %collective-permute-done.rest_0_, bf16[32,6272]{1,0:T(8,128)(2,1)S(1)} %collective-permute-done.1.rest_1_), custom_call_target="tpu_custom_call" | custom-call | flops 205520896 | bytes 1024 | tf_op jit(solution)/shard_map/pallas_call | solution.py:302
  39.5 1.9 collective-permute-done.2.rest_0_
  42.7 11.6 %all_to_all.41.partials = f32[8,32,256]{2,1,0:T(8,128)S(1)} all-to-all(f32[8,32,256]{2,1,0:T(8,128)S(1)} %shard_map.50), channel_id=1, replica_groups=mesh['za'=4,'zb'=2,'ya'=2,'yb'=2,'feat'=8] {'feat'}, dimensions={0} | all-to-all | bytes 524288 | tf_op jit(solution)/shard_map/all_to_all | solution.py:314
  54.6 15.0 %all_to_all.42.grams = f32[32,8,128]{2,1,0:T(8,128)S(1)} all-to-all(f32[32,8,128]{2,1,0:T(8,128)S(1)} %get-tuple-element.29), channel_id=1, replica_groups=mesh['za'=4,'zb'=2,'ya'=2,'yb'=2,'feat'=8] {'za','zb','ya','yb'}, dimensions={0} | all-to-all | bytes 262144 | tf_op jit(solution)/shard_map/all_to_all | solution.py:314
  71.3 2.2 %collective-permute-start.3 = (bf16[32,6272]{1,0:T(8,128)(2,1)S(1)}, bf16[32,6272]{1,0:T(8,128)(2,1)S(1)}, u32[]{:S(2)}, u32[]{:S(2)}) collective-permute-start(bf16[32,6272]{1,0:T(8,128)(2,1)S(1)} %get-tuple-element.33), channel_id=1, source_target_pairs={{0,40},{1,249},{2,42},{3,251},{4,44},{5,253},{6,46},{7,255},{8,32}... | collective-permute-start | bytes 1204232 | tf_op jit(solution)/shard_map/ppermute | solution.py:86
  76.3 4.0 %collective-permute-done.3.received = bf16[32,6272]{1,0:T(8,128)(2,1)S(1)} collective-permute-done((bf16[32,6272]{1,0:T(8,128)(2,1)S(1)}, bf16[32,6272]{1,0:T(8,128)(2,1)S(1)}, u32[]{:S(2)}, u32[]{:S(2)}) %collective-permute-start.3) | collective-permute-done | bytes 401440 | tf_op jit(solution)/shard_map/ppermute | solution.py:86
  81.0 4.0 %collective-permute-done.4.rest_0_ = bf16[32,6272]{1,0:T(8,128)(2,1)S(1)} collective-permute-done((bf16[32,6272]{1,0:T(8,128)(2,1)S(1)}, bf16[32,6272]{1,0:T(8,128)(2,1)S(1)}, u32[]{:S(2)}, u32[]{:S(2)}) %collective-permute-start.4) | collective-permute-done | bytes 401440 | tf_op jit(solution)/shard_map/ppermute | solution.py:86
  85.1 18.9 %all_to_all.43.windows = bf16[8,32,896]{2,1,0:T(8,128)(2,1)S(1)} all-to-all(bf16[8,32,896]{2,1,0:T(8,128)(2,1)S(1)} %shard_map.55), channel_id=1, replica_groups=mesh['za'=4,'zb'=2,'ya'=2,'yb'=2,'feat'=8] {'za','ya'}, dimensions={0} | all-to-all | bytes 917504 | tf_op jit(solution)/shard_map/all_to_all | solution.py:314
  104.3 19.1 %all_to_all.44.windows = bf16[8,32,896]{2,1,0:T(8,128)(2,1)S(1)} all-to-all(bf16[8,32,896]{2,1,0:T(8,128)(2,1)S(1)} %get-tuple-element.36), channel_id=1, replica_groups=mesh['za'=4,'zb'=2,'ya'=2,'yb'=2,'feat'=8] {'za','ya'}, dimensions={0} | all-to-all | bytes 917504 | tf_op jit(solution)/shard_map/all_to_all | solution.py:314
  124.1 1.8 collective-permute-start.6
  128.4 3.1 %collective-permute-done.7.rest_1_ = bf16[32,6272]{1,0:T(8,128)(2,1)S(1)} collective-permute-done((bf16[32,6272]{1,0:T(8,128)(2,1)S(1)}, bf16[32,6272]{1,0:T(8,128)(2,1)S(1)}, u32[]{:S(2)}, u32[]{:S(2)}) %collective-permute-start.7) | collective-permute-done | bytes 401440 | tf_op jit(solution)/shard_map/ppermute | solution.py:86
  131.9 2.2 %shard_map.59.before = f32[256,32]{1,0:T(8,128)S(1)} custom-call(bf16[256,25088]{1,0:T(8,128)(2,1)S(1)} %get-tuple-element.27.features, f32[256,32]{1,0:T(8,128)S(1)} %shard_map.58.before, bf16[32,6272]{1,0:T(8,128)(2,1)S(1)} %collective-permute-done.6.rest_0_, bf16[32,6272]{1,0:T(8,128)(2,1)S(1)} %collective-permute-done.7.rest_1_), custom_call_target="tpu_custom_call" | custom-call | flops 205520896 | bytes 1024 | tf_op jit(solution)/shard_map/pallas_call | solution.py:302
  134.1 3.2 %collective-permute-done.8.rest_0_ = bf16[32,6272]{1,0:T(8,128)(2,1)S(1)} collective-permute-done((bf16[32,6272]{1,0:T(8,128)(2,1)S(1)}, bf16[32,6272]{1,0:T(8,128)(2,1)S(1)}, u32[]{:S(2)}, u32[]{:S(2)}) %collective-permute-start.8) | collective-permute-done | bytes 401440 | tf_op jit(solution)/shard_map/ppermute | solution.py:86
  138.6 9.9 %all_to_all.45.partials = f32[8,32,256]{2,1,0:T(8,128)S(1)} all-to-all(f32[8,32,256]{2,1,0:T(8,128)S(1)} %shard_map.60), channel_id=1, replica_groups=mesh['za'=4,'zb'=2,'ya'=2,'yb'=2,'feat'=8] {'feat'}, dimensions={0} | all-to-all | bytes 524288 | tf_op jit(solution)/shard_map/all_to_all | solution.py:314
  148.8 13.9 %all_to_all.46.grams = f32[32,8,128]{2,1,0:T(8,128)S(1)} all-to-all(f32[32,8,128]{2,1,0:T(8,128)S(1)} %get-tuple-element.37), channel_id=1, replica_groups=mesh['za'=4,'zb'=2,'ya'=2,'yb'=2,'feat'=8] {'za','zb','ya','yb'}, dimensions={0} | all-to-all | bytes 262144 | tf_op jit(solution)/shard_map/all_to_all | solution.py:314
  162.7 1.7 shard_map.62
  164.5 2.2 %collective-permute-start.9 = (bf16[32,6272]{1,0:T(8,128)(2,1)S(1)}, bf16[32,6272]{1,0:T(8,128)(2,1)S(1)}, u32[]{:S(2)}, u32[]{:S(2)}) collective-permute-start(bf16[32,6272]{1,0:T(8,128)(2,1)S(1)} %get-tuple-element.41), channel_id=1, source_target_pairs={{0,40},{1,249},{2,42},{3,251},{4,44},{5,253},{6,46},{7,255},{8,32}... | collective-permute-start | bytes 1204232 | tf_op jit(solution)/shard_map/ppermute | solution.py:86
  169.4 4.0 %collective-permute-done.9.received = bf16[32,6272]{1,0:T(8,128)(2,1)S(1)} collective-permute-done((bf16[32,6272]{1,0:T(8,128)(2,1)S(1)}, bf16[32,6272]{1,0:T(8,128)(2,1)S(1)}, u32[]{:S(2)}, u32[]{:S(2)}) %collective-permute-start.9) | collective-permute-done | bytes 401440 | tf_op jit(solution)/shard_map/ppermute | solution.py:86
  174.1 4.0 %collective-permute-done.10.rest_0_ = bf16[32,6272]{1,0:T(8,128)(2,1)S(1)} collective-permute-done((bf16[32,6272]{1,0:T(8,128)(2,1)S(1)}, bf16[32,6272]{1,0:T(8,128)(2,1)S(1)}, u32[]{:S(2)}, u32[]{:S(2)}) %collective-permute-start.10) | collective-permute-done | bytes 401440 | tf_op jit(solution)/shard_map/ppermute | solution.py:86
  178.2 18.9 %all_to_all.47.windows = bf16[8,32,896]{2,1,0:T(8,128)(2,1)S(1)} all-to-all(bf16[8,32,896]{2,1,0:T(8,128)(2,1)S(1)} %shard_map.65), channel_id=1, replica_groups=mesh['za'=4,'zb'=2,'ya'=2,'yb'=2,'feat'=8] {'za','ya'}, dimensions={0} | all-to-all | bytes 917504 | tf_op jit(solution)/shard_map/all_to_all | solution.py:314
  (33 shorter events, 18.2 us)
Async XLA Ops:
  27.7 9.6 %collective-permute-start.1 = (bf16[32,6272]{1,0:T(8,128)(2,1)S(1)}, bf16[32,6272]{1,0:T(8,128)(2,1)S(1)}, u32[]{:S(2)}, u32[]{:S(2)}) collective-permute-start(bf16[32,6272]{1,0:T(8,128)(2,1)S(1)} %shard_map.47.joined), channel_id=1, source_target_pairs={{0,8},{1,25},{2,10},{3,27},{4,12},{5,29},{6,14},{7,31},{8,0},{9,17... | collective-permute-start | bytes 1204232 | tf_op jit(solution)/shard_map/ppermute | solution.py:86
  29.1 8.2 %collective-permute-start = (bf16[32,6272]{1,0:T(8,128)(2,1)S(1)}, bf16[32,6272]{1,0:T(8,128)(2,1)S(1)}, u32[]{:S(2)}, u32[]{:S(2)}) collective-permute-start(bf16[32,6272]{1,0:T(8,128)(2,1)S(1)} %shard_map.47.joined), channel_id=1, source_target_pairs={{0,32},{1,225},{2,34},{3,227},{4,36},{5,229},{6,38},{7,231},{8,40}... | collective-permute-start | bytes 1204232 | tf_op jit(solution)/shard_map/ppermute | solution.py:86
  31.1 10.3 %collective-permute-start.2 = (bf16[32,6272]{1,0:T(8,128)(2,1)S(1)}, bf16[32,6272]{1,0:T(8,128)(2,1)S(1)}, u32[]{:S(2)}, u32[]{:S(2)}) collective-permute-start(bf16[32,6272]{1,0:T(8,128)(2,1)S(1)} %shard_map.47.joined), channel_id=1, source_target_pairs={{0,40},{1,249},{2,42},{3,251},{4,44},{5,253},{6,46},{7,255},{8,32}... | collective-permute-start | bytes 1204232 | tf_op jit(solution)/shard_map/ppermute | solution.py:86
  71.3 8.9 %collective-permute-start.3 = (bf16[32,6272]{1,0:T(8,128)(2,1)S(1)}, bf16[32,6272]{1,0:T(8,128)(2,1)S(1)}, u32[]{:S(2)}, u32[]{:S(2)}) collective-permute-start(bf16[32,6272]{1,0:T(8,128)(2,1)S(1)} %get-tuple-element.33), channel_id=1, source_target_pairs={{0,40},{1,249},{2,42},{3,251},{4,44},{5,253},{6,46},{7,255},{8,32}... | collective-permute-start | bytes 1204232 | tf_op jit(solution)/shard_map/ppermute | solution.py:86
  73.6 30.5 %copy-start = (f32[1,32,784]{2,1,0:T(8,128)S(1)}, f32[1,32,784]{2,1,0:T(8,128)}, u32[]{:S(2)}) copy-start(f32[1,32,784]{2,1,0:T(8,128)} %param.5) | copy-start | bytes 301060
  73.6 30.5 %copy-start.1 = (f32[32,784]{1,0:T(8,128)S(1)}, f32[32,784]{1,0:T(8,128)}, u32[]{:S(2)}) copy-start(f32[32,784]{1,0:T(8,128)} %get-tuple-element.25.mask) | copy-start | bytes 301060
  74.8 10.1 %collective-permute-start.4 = (bf16[32,6272]{1,0:T(8,128)(2,1)S(1)}, bf16[32,6272]{1,0:T(8,128)(2,1)S(1)}, u32[]{:S(2)}, u32[]{:S(2)}) collective-permute-start(bf16[32,6272]{1,0:T(8,128)(2,1)S(1)} %get-tuple-element.34), channel_id=1, source_target_pairs={{0,32},{1,225},{2,34},{3,227},{4,36},{5,229},{6,38},{7,231},{8,40}... | collective-permute-start | bytes 1204232 | tf_op jit(solution)/shard_map/ppermute | solution.py:86
  76.2 8.8 %collective-permute-start.5 = (bf16[32,6272]{1,0:T(8,128)(2,1)S(1)}, bf16[32,6272]{1,0:T(8,128)(2,1)S(1)}, u32[]{:S(2)}, u32[]{:S(2)}) collective-permute-start(bf16[32,6272]{1,0:T(8,128)(2,1)S(1)} %get-tuple-element.35), channel_id=1, source_target_pairs={{0,8},{1,25},{2,10},{3,27},{4,12},{5,29},{6,14},{7,31},{8,0},{9,17... | collective-permute-start | bytes 1204232 | tf_op jit(solution)/shard_map/ppermute | solution.py:86
  123.4 8.1 %collective-permute-start.7 = (bf16[32,6272]{1,0:T(8,128)(2,1)S(1)}, bf16[32,6272]{1,0:T(8,128)(2,1)S(1)}, u32[]{:S(2)}, u32[]{:S(2)}) collective-permute-start(bf16[32,6272]{1,0:T(8,128)(2,1)S(1)} %shard_map.57.rest_0_), channel_id=1, source_target_pairs={{0,8},{1,25},{2,10},{3,27},{4,12},{5,29},{6,14},{7,31},{8,0},{9,17... | collective-permute-start | bytes 1204232 | tf_op jit(solution)/shard_map/ppermute | solution.py:86
  124.1 7.9 %collective-permute-start.6 = (bf16[32,6272]{1,0:T(8,128)(2,1)S(1)}, bf16[32,6272]{1,0:T(8,128)(2,1)S(1)}, u32[]{:S(2)}, u32[]{:S(2)}) collective-permute-start(bf16[32,6272]{1,0:T(8,128)(2,1)S(1)} %shard_map.57.rest_0_), channel_id=1, source_target_pairs={{0,32},{1,225},{2,34},{3,227},{4,36},{5,229},{6,38},{7,231},{8,40}... | collective-permute-start | bytes 1204232 | tf_op jit(solution)/shard_map/ppermute | solution.py:86
  125.9 11.5 %collective-permute-start.8 = (bf16[32,6272]{1,0:T(8,128)(2,1)S(1)}, bf16[32,6272]{1,0:T(8,128)(2,1)S(1)}, u32[]{:S(2)}, u32[]{:S(2)}) collective-permute-start(bf16[32,6272]{1,0:T(8,128)(2,1)S(1)} %shard_map.57.rest_0_), channel_id=1, source_target_pairs={{0,40},{1,249},{2,42},{3,251},{4,44},{5,253},{6,46},{7,255},{8,32}... | collective-permute-start | bytes 1204232 | tf_op jit(solution)/shard_map/ppermute | solution.py:86
  164.5 8.9 %collective-permute-start.9 = (bf16[32,6272]{1,0:T(8,128)(2,1)S(1)}, bf16[32,6272]{1,0:T(8,128)(2,1)S(1)}, u32[]{:S(2)}, u32[]{:S(2)}) collective-permute-start(bf16[32,6272]{1,0:T(8,128)(2,1)S(1)} %get-tuple-element.41), channel_id=1, source_target_pairs={{0,40},{1,249},{2,42},{3,251},{4,44},{5,253},{6,46},{7,255},{8,32}... | collective-permute-start | bytes 1204232 | tf_op jit(solution)/shard_map/ppermute | solution.py:86
  168.0 10.1 %collective-permute-start.10 = (bf16[32,6272]{1,0:T(8,128)(2,1)S(1)}, bf16[32,6272]{1,0:T(8,128)(2,1)S(1)}, u32[]{:S(2)}, u32[]{:S(2)}) collective-permute-start(bf16[32,6272]{1,0:T(8,128)(2,1)S(1)} %get-tuple-element.42), channel_id=1, source_target_pairs={{0,32},{1,225},{2,34},{3,227},{4,36},{5,229},{6,38},{7,231},{8,40}... | collective-permute-start | bytes 1204232 | tf_op jit(solution)/shard_map/ppermute | solution.py:86
  169.3 8.8 %collective-permute-start.11 = (bf16[32,6272]{1,0:T(8,128)(2,1)S(1)}, bf16[32,6272]{1,0:T(8,128)(2,1)S(1)}, u32[]{:S(2)}, u32[]{:S(2)}) collective-permute-start(bf16[32,6272]{1,0:T(8,128)(2,1)S(1)} %get-tuple-element.43), channel_id=1, source_target_pairs={{0,8},{1,25},{2,10},{3,27},{4,12},{5,29},{6,14},{7,31},{8,0},{9,17... | collective-permute-start | bytes 1204232 | tf_op jit(solution)/shard_map/ppermute | solution.py:86

commit v2 on v1

--- a/solution.py
+++ b/solution.py
@@ -12,7 +12,7 @@
 K = 32
 ITERS = 2
 LANES = 128
-STEPS = ((1, 0), (0, 1), (1, 1))
+STEPS = ((0, 1), (1, 0), (1, 1))
 HERE = (0, 0)
 FAR = ("za", "ya")
 DOM = ("za", "zb", "ya", "yb")
@@ -137,8 +137,8 @@
             weights = piece[:, start : start + size].astype(F32)
             weights = moved(weights, part * width % LANES, begin, width).astype(BF16)
             product = lax.dot_general(
+                weights,
                 features[:, columns],
-                weights,
                 (((1,), (1,)), ((), ())),
                 preferred_element_type=F32,
             )
@@ -172,7 +172,7 @@
 
 def project_last_kernel(far, steps, features, before, *rest):
     *pieces, copies = rest
-    total = projected(far, steps, pieces, features, before[...]).T
+    total = projected(far, steps, pieces, features, before[...])
     for copy in range(copies.shape[0]):
         copies[copy] = total
 
@@ -331,7 +331,7 @@
     line = ((far, K, size), BF16)
     message = ((K, joined_size), BF16)
     rows = ((K, row_count), F32)
-    total = ((row_count, K), F32)
+    total = ((K, row_count), F32)
     partial = ((feats, K, row_count), F32)
     piece_flops = 2 * row_count * K * joined_size
 
@@ -398,8 +398,10 @@
             held,
         )
         first = send(made, STEPS[2])
-        made = messages(residual, held, STEPS[:2])
-        received = [send(item, step) for item, step in zip(made, STEPS[:2])]
+        received = []
+        for step in STEPS[1::-1]:
+            (made,) = messages(residual, held, (step,))
+            received.append(send(made, step))
         kernel = functools.partial(kept_kernel, far)
         (kept,) = call(
             kernel, [(message[0], F32)], [], [VMEM] * 3, residual, held, first, flops=piece_flops * 8

time: 198 us -> 198 us (level)
    pallas_call x21 -> x23, Pallas kernels: 25.4 us -> 26.1 us  [call(): pl.pallas_call(kernel, out_shape=shapes, in_specs=specs, out_specs=tuple(...]
where the time goes in v2:
time: 198 us
  blocking collectives  133 us (67%)
  Pallas kernels  26.1 us (13%)
  waiting for transfers between devices  23.8 us (12%)
  starting transfers between devices  14.5 us (7%)
    all_to_all x8, blocking collectives, exchange(): return lax.all_to_all(copies, axis, 0, 0, tiled=True)  133 us
    pallas_call x23, Pallas kernels, call(): pl.pallas_call(kernel, out_shape=shapes, in_specs=specs, out_specs=tuple(...  26.1 us
    ppermute x12, waiting for transfers between devices, send(): lax.ppermute(message, AXES, route(step, zs, ys, lax.axis_size('feat')))  23.8 us
    ppermute x12, starting transfers between devices, send(): lax.ppermute(message, AXES, route(step, zs, ys, lax.axis_size('feat')))  14.5 us
  transfers between devices with their start and end apart: 12, of which 8 were waited for; matrix products, arithmetic and copies ran while one was open for 0% of the time, Pallas kernels for 8%

profile of v2, /device:TPU:8, one launch (start us, length us, event | category | flops | bytes accessed | tf_op | source)
XLA Modules:
  0.0 197.7 jit_solution(8892027286314547332)
XLA Ops:
  0.0 1.8 shard_map.46
  1.8 25.8 %all_to_all.40.windows = bf16[8,32,896]{2,1,0:T(8,128)(2,1)S(1)} all-to-all(bf16[8,32,896]{2,1,0:T(8,128)(2,1)} %get-tuple-element.22), channel_id=1, replica_groups=mesh['za'=4,'zb'=2,'ya'=2,'yb'=2,'feat'=8] {'za','ya'}, dimensions={0} | all-to-all | bytes 917504 | tf_op jit(solution)/shard_map/all_to_all | solution.py:314
  29.1 2.0 %collective-permute-start.1 = (bf16[32,6272]{1,0:T(8,128)(2,1)S(1)}, bf16[32,6272]{1,0:T(8,128)(2,1)S(1)}, u32[]{:S(2)}, u32[]{:S(2)}) collective-permute-start(bf16[32,6272]{1,0:T(8,128)(2,1)S(1)} %shard_map.47.joined), channel_id=1, source_target_pairs={{0,32},{1,225},{2,34},{3,227},{4,36},{5,229},{6,38},{7,231},{8,40}... | collective-permute-start | bytes 1204232 | tf_op jit(solution)/shard_map/ppermute | solution.py:86
  31.3 6.0 %shard_map.48 = (f32[32,256]{1,0:T(8,128)S(1)}, bf16[256,25088]{1,0:T(8,128)(2,1)S(1)}) custom-call(bf16[256,25088]{1,0:T(8,128)(2,1)} %bitcast.5, bf16[32,6272]{1,0:T(8,128)(2,1)S(1)} %shard_map.47.joined), custom_call_target="tpu_custom_call" | custom-call | flops 102760448 | bytes 1024 | tf_op jit(solution)/shard_map/pallas_call | solution.py:302
  37.3 2.3 %shard_map.49.before = f32[32,256]{1,0:T(8,128)S(1)} custom-call(bf16[256,25088]{1,0:T(8,128)(2,1)S(1)} %get-tuple-element.23.features, f32[32,256]{1,0:T(8,128)S(1)} %get-tuple-element.24.before, bf16[32,6272]{1,0:T(8,128)(2,1)S(1)} %collective-permute-done.rest_0_, bf16[32,6272]{1,0:T(8,128)(2,1)S(1)} %collective-permute-done.1.rest_1_), custom_call_target="tpu_custom_call" | custom-call | flops 205520896 | bytes 1024 | tf_op jit(solution)/shard_map/pallas_call | solution.py:302
  42.7 11.6 %all_to_all.41.partials = f32[8,32,256]{2,1,0:T(8,128)S(1)} all-to-all(f32[8,32,256]{2,1,0:T(8,128)S(1)} %shard_map.50), channel_id=1, replica_groups=mesh['za'=4,'zb'=2,'ya'=2,'yb'=2,'feat'=8] {'feat'}, dimensions={0} | all-to-all | bytes 524288 | tf_op jit(solution)/shard_map/all_to_all | solution.py:314
  54.6 15.0 %all_to_all.42.grams = f32[32,8,128]{2,1,0:T(8,128)S(1)} all-to-all(f32[32,8,128]{2,1,0:T(8,128)S(1)} %get-tuple-element.25), channel_id=1, replica_groups=mesh['za'=4,'zb'=2,'ya'=2,'yb'=2,'feat'=8] {'za','zb','ya','yb'}, dimensions={0} | all-to-all | bytes 262144 | tf_op jit(solution)/shard_map/all_to_all | solution.py:314
  69.6 1.7 shard_map.52
  71.3 2.2 %collective-permute-start.3 = (bf16[32,6272]{1,0:T(8,128)(2,1)S(1)}, bf16[32,6272]{1,0:T(8,128)(2,1)S(1)}, u32[]{:S(2)}, u32[]{:S(2)}) collective-permute-start(bf16[32,6272]{1,0:T(8,128)(2,1)S(1)} %get-tuple-element.29), channel_id=1, source_target_pairs={{0,40},{1,249},{2,42},{3,251},{4,44},{5,253},{6,46},{7,255},{8,32}... | collective-permute-start | bytes 1204232 | tf_op jit(solution)/shard_map/ppermute | solution.py:86
  76.5 3.7 %collective-permute-done.3.received = bf16[32,6272]{1,0:T(8,128)(2,1)S(1)} collective-permute-done((bf16[32,6272]{1,0:T(8,128)(2,1)S(1)}, bf16[32,6272]{1,0:T(8,128)(2,1)S(1)}, u32[]{:S(2)}, u32[]{:S(2)}) %collective-permute-start.3) | collective-permute-done | bytes 401440 | tf_op jit(solution)/shard_map/ppermute | solution.py:86
  80.9 4.0 %collective-permute-done.4.rest_0_ = bf16[32,6272]{1,0:T(8,128)(2,1)S(1)} collective-permute-done((bf16[32,6272]{1,0:T(8,128)(2,1)S(1)}, bf16[32,6272]{1,0:T(8,128)(2,1)S(1)}, u32[]{:S(2)}, u32[]{:S(2)}) %collective-permute-start.4) | collective-permute-done | bytes 401440 | tf_op jit(solution)/shard_map/ppermute | solution.py:86
  85.1 18.9 %all_to_all.43.windows = bf16[8,32,896]{2,1,0:T(8,128)(2,1)S(1)} all-to-all(bf16[8,32,896]{2,1,0:T(8,128)(2,1)S(1)} %shard_map.56), channel_id=1, replica_groups=mesh['za'=4,'zb'=2,'ya'=2,'yb'=2,'feat'=8] {'za','ya'}, dimensions={0} | all-to-all | bytes 917504 | tf_op jit(solution)/shard_map/all_to_all | solution.py:314
  104.3 19.1 %all_to_all.44.windows = bf16[8,32,896]{2,1,0:T(8,128)(2,1)S(1)} all-to-all(bf16[8,32,896]{2,1,0:T(8,128)(2,1)S(1)} %get-tuple-element.30), channel_id=1, replica_groups=mesh['za'=4,'zb'=2,'ya'=2,'yb'=2,'feat'=8] {'za','ya'}, dimensions={0} | all-to-all | bytes 917504 | tf_op jit(solution)/shard_map/all_to_all | solution.py:314
  123.9 1.8 collective-permute-start.7
  128.2 3.1 %collective-permute-done.6.rest_0_ = bf16[32,6272]{1,0:T(8,128)(2,1)S(1)} collective-permute-done((bf16[32,6272]{1,0:T(8,128)(2,1)S(1)}, bf16[32,6272]{1,0:T(8,128)(2,1)S(1)}, u32[]{:S(2)}, u32[]{:S(2)}) %collective-permute-start.6) | collective-permute-done | bytes 401440 | tf_op jit(solution)/shard_map/ppermute | solution.py:86
  131.8 2.3 %shard_map.60.before = f32[32,256]{1,0:T(8,128)S(1)} custom-call(bf16[256,25088]{1,0:T(8,128)(2,1)S(1)} %get-tuple-element.23.features, f32[32,256]{1,0:T(8,128)S(1)} %shard_map.59.before, bf16[32,6272]{1,0:T(8,128)(2,1)S(1)} %collective-permute-done.6.rest_0_, bf16[32,6272]{1,0:T(8,128)(2,1)S(1)} %collective-permute-done.7.rest_1_), custom_call_target="tpu_custom_call" | custom-call | flops 205520896 | bytes 1024 | tf_op jit(solution)/shard_map/pallas_call | solution.py:302
  134.1 3.0 %collective-permute-done.8.rest_0_ = bf16[32,6272]{1,0:T(8,128)(2,1)S(1)} collective-permute-done((bf16[32,6272]{1,0:T(8,128)(2,1)S(1)}, bf16[32,6272]{1,0:T(8,128)(2,1)S(1)}, u32[]{:S(2)}, u32[]{:S(2)}) %collective-permute-start.8) | collective-permute-done | bytes 401440 | tf_op jit(solution)/shard_map/ppermute | solution.py:86
  138.4 9.9 %all_to_all.45.partials = f32[8,32,256]{2,1,0:T(8,128)S(1)} all-to-all(f32[8,32,256]{2,1,0:T(8,128)S(1)} %shard_map.61), channel_id=1, replica_groups=mesh['za'=4,'zb'=2,'ya'=2,'yb'=2,'feat'=8] {'feat'}, dimensions={0} | all-to-all | bytes 524288 | tf_op jit(solution)/shard_map/all_to_all | solution.py:314
  148.6 13.9 %all_to_all.46.grams = f32[32,8,128]{2,1,0:T(8,128)S(1)} all-to-all(f32[32,8,128]{2,1,0:T(8,128)S(1)} %get-tuple-element.31), channel_id=1, replica_groups=mesh['za'=4,'zb'=2,'ya'=2,'yb'=2,'feat'=8] {'za','zb','ya','yb'}, dimensions={0} | all-to-all | bytes 262144 | tf_op jit(solution)/shard_map/all_to_all | solution.py:314
  162.5 1.7 shard_map.63
  164.2 2.2 %collective-permute-start.9 = (bf16[32,6272]{1,0:T(8,128)(2,1)S(1)}, bf16[32,6272]{1,0:T(8,128)(2,1)S(1)}, u32[]{:S(2)}, u32[]{:S(2)}) collective-permute-start(bf16[32,6272]{1,0:T(8,128)(2,1)S(1)} %get-tuple-element.35), channel_id=1, source_target_pairs={{0,40},{1,249},{2,42},{3,251},{4,44},{5,253},{6,46},{7,255},{8,32}... | collective-permute-start | bytes 1204232 | tf_op jit(solution)/shard_map/ppermute | solution.py:86
  169.4 3.7 %collective-permute-done.9.received = bf16[32,6272]{1,0:T(8,128)(2,1)S(1)} collective-permute-done((bf16[32,6272]{1,0:T(8,128)(2,1)S(1)}, bf16[32,6272]{1,0:T(8,128)(2,1)S(1)}, u32[]{:S(2)}, u32[]{:S(2)}) %collective-permute-start.9) | collective-permute-done | bytes 401440 | tf_op jit(solution)/shard_map/ppermute | solution.py:86
  173.9 4.0 %collective-permute-done.10.rest_0_ = bf16[32,6272]{1,0:T(8,128)(2,1)S(1)} collective-permute-done((bf16[32,6272]{1,0:T(8,128)(2,1)S(1)}, bf16[32,6272]{1,0:T(8,128)(2,1)S(1)}, u32[]{:S(2)}, u32[]{:S(2)}) %collective-permute-start.10) | collective-permute-done | bytes 401440 | tf_op jit(solution)/shard_map/ppermute | solution.py:86
  178.0 18.9 %all_to_all.47.windows = bf16[8,32,896]{2,1,0:T(8,128)(2,1)S(1)} all-to-all(bf16[8,32,896]{2,1,0:T(8,128)(2,1)S(1)} %shard_map.67), channel_id=1, replica_groups=mesh['za'=4,'zb'=2,'ya'=2,'yb'=2,'feat'=8] {'za','ya'}, dimensions={0} | all-to-all | bytes 917504 | tf_op jit(solution)/shard_map/all_to_all | solution.py:314
  (35 shorter events, 18.5 us)
Async XLA Ops:
  27.7 9.6 %collective-permute-start = (bf16[32,6272]{1,0:T(8,128)(2,1)S(1)}, bf16[32,6272]{1,0:T(8,128)(2,1)S(1)}, u32[]{:S(2)}, u32[]{:S(2)}) collective-permute-start(bf16[32,6272]{1,0:T(8,128)(2,1)S(1)} %shard_map.47.joined), channel_id=1, source_target_pairs={{0,8},{1,25},{2,10},{3,27},{4,12},{5,29},{6,14},{7,31},{8,0},{9,17... | collective-permute-start | bytes 1204232 | tf_op jit(solution)/shard_map/ppermute | solution.py:86
  29.1 8.2 %collective-permute-start.1 = (bf16[32,6272]{1,0:T(8,128)(2,1)S(1)}, bf16[32,6272]{1,0:T(8,128)(2,1)S(1)}, u32[]{:S(2)}, u32[]{:S(2)}) collective-permute-start(bf16[32,6272]{1,0:T(8,128)(2,1)S(1)} %shard_map.47.joined), channel_id=1, source_target_pairs={{0,32},{1,225},{2,34},{3,227},{4,36},{5,229},{6,38},{7,231},{8,40}... | collective-permute-start | bytes 1204232 | tf_op jit(solution)/shard_map/ppermute | solution.py:86
  31.1 10.3 %collective-permute-start.2 = (bf16[32,6272]{1,0:T(8,128)(2,1)S(1)}, bf16[32,6272]{1,0:T(8,128)(2,1)S(1)}, u32[]{:S(2)}, u32[]{:S(2)}) collective-permute-start(bf16[32,6272]{1,0:T(8,128)(2,1)S(1)} %shard_map.47.joined), channel_id=1, source_target_pairs={{0,40},{1,249},{2,42},{3,251},{4,44},{5,253},{6,46},{7,255},{8,32}... | collective-permute-start | bytes 1204232 | tf_op jit(solution)/shard_map/ppermute | solution.py:86
  71.3 8.9 %collective-permute-start.3 = (bf16[32,6272]{1,0:T(8,128)(2,1)S(1)}, bf16[32,6272]{1,0:T(8,128)(2,1)S(1)}, u32[]{:S(2)}, u32[]{:S(2)}) collective-permute-start(bf16[32,6272]{1,0:T(8,128)(2,1)S(1)} %get-tuple-element.29), channel_id=1, source_target_pairs={{0,40},{1,249},{2,42},{3,251},{4,44},{5,253},{6,46},{7,255},{8,32}... | collective-permute-start | bytes 1204232 | tf_op jit(solution)/shard_map/ppermute | solution.py:86
  74.3 29.7 %copy-start = (f32[1,32,784]{2,1,0:T(8,128)S(1)}, f32[1,32,784]{2,1,0:T(8,128)}, u32[]{:S(2)}) copy-start(f32[1,32,784]{2,1,0:T(8,128)} %param.5) | copy-start | bytes 301060
  74.3 29.7 %copy-start.1 = (f32[32,784]{1,0:T(8,128)S(1)}, f32[32,784]{1,0:T(8,128)}, u32[]{:S(2)}) copy-start(f32[32,784]{1,0:T(8,128)} %get-tuple-element.21.mask) | copy-start | bytes 301060
  75.1 9.9 %collective-permute-start.4 = (bf16[32,6272]{1,0:T(8,128)(2,1)S(1)}, bf16[32,6272]{1,0:T(8,128)(2,1)S(1)}, u32[]{:S(2)}, u32[]{:S(2)}) collective-permute-start(bf16[32,6272]{1,0:T(8,128)(2,1)S(1)} %shard_map.54), channel_id=1, source_target_pairs={{0,32},{1,225},{2,34},{3,227},{4,36},{5,229},{6,38},{7,231},{8,40}... | collective-permute-start | bytes 1204232 | tf_op jit(solution)/shard_map/ppermute | solution.py:86
  76.4 8.6 %collective-permute-start.5 = (bf16[32,6272]{1,0:T(8,128)(2,1)S(1)}, bf16[32,6272]{1,0:T(8,128)(2,1)S(1)}, u32[]{:S(2)}, u32[]{:S(2)}) collective-permute-start(bf16[32,6272]{1,0:T(8,128)(2,1)S(1)} %shard_map.55), channel_id=1, source_target_pairs={{0,8},{1,25},{2,10},{3,27},{4,12},{5,29},{6,14},{7,31},{8,0},{9,17... | collective-permute-start | bytes 1204232 | tf_op jit(solution)/shard_map/ppermute | solution.py:86
  123.4 8.0 %collective-permute-start.6 = (bf16[32,6272]{1,0:T(8,128)(2,1)S(1)}, bf16[32,6272]{1,0:T(8,128)(2,1)S(1)}, u32[]{:S(2)}, u32[]{:S(2)}) collective-permute-start(bf16[32,6272]{1,0:T(8,128)(2,1)S(1)} %shard_map.58.rest_0_), channel_id=1, source_target_pairs={{0,8},{1,25},{2,10},{3,27},{4,12},{5,29},{6,14},{7,31},{8,0},{9,17... | collective-permute-start | bytes 1204232 | tf_op jit(solution)/shard_map/ppermute | solution.py:86
  123.9 7.9 %collective-permute-start.7 = (bf16[32,6272]{1,0:T(8,128)(2,1)S(1)}, bf16[32,6272]{1,0:T(8,128)(2,1)S(1)}, u32[]{:S(2)}, u32[]{:S(2)}) collective-permute-start(bf16[32,6272]{1,0:T(8,128)(2,1)S(1)} %shard_map.58.rest_0_), channel_id=1, source_target_pairs={{0,32},{1,225},{2,34},{3,227},{4,36},{5,229},{6,38},{7,231},{8,40}... | collective-permute-start | bytes 1204232 | tf_op jit(solution)/shard_map/ppermute | solution.py:86
  125.7 11.5 %collective-permute-start.8 = (bf16[32,6272]{1,0:T(8,128)(2,1)S(1)}, bf16[32,6272]{1,0:T(8,128)(2,1)S(1)}, u32[]{:S(2)}, u32[]{:S(2)}) collective-permute-start(bf16[32,6272]{1,0:T(8,128)(2,1)S(1)} %shard_map.58.rest_0_), channel_id=1, source_target_pairs={{0,40},{1,249},{2,42},{3,251},{4,44},{5,253},{6,46},{7,255},{8,32}... | collective-permute-start | bytes 1204232 | tf_op jit(solution)/shard_map/ppermute | solution.py:86
  164.2 8.9 %collective-permute-start.9 = (bf16[32,6272]{1,0:T(8,128)(2,1)S(1)}, bf16[32,6272]{1,0:T(8,128)(2,1)S(1)}, u32[]{:S(2)}, u32[]{:S(2)}) collective-permute-start(bf16[32,6272]{1,0:T(8,128)(2,1)S(1)} %get-tuple-element.35), channel_id=1, source_target_pairs={{0,40},{1,249},{2,42},{3,251},{4,44},{5,253},{6,46},{7,255},{8,32}... | collective-permute-start | bytes 1204232 | tf_op jit(solution)/shard_map/ppermute | solution.py:86
  168.0 9.9 %collective-permute-start.10 = (bf16[32,6272]{1,0:T(8,128)(2,1)S(1)}, bf16[32,6272]{1,0:T(8,128)(2,1)S(1)}, u32[]{:S(2)}, u32[]{:S(2)}) collective-permute-start(bf16[32,6272]{1,0:T(8,128)(2,1)S(1)} %shard_map.65), channel_id=1, source_target_pairs={{0,32},{1,225},{2,34},{3,227},{4,36},{5,229},{6,38},{7,231},{8,40}... | collective-permute-start | bytes 1204232 | tf_op jit(solution)/shard_map/ppermute | solution.py:86
  169.3 8.6 %collective-permute-start.11 = (bf16[32,6272]{1,0:T(8,128)(2,1)S(1)}, bf16[32,6272]{1,0:T(8,128)(2,1)S(1)}, u32[]{:S(2)}, u32[]{:S(2)}) collective-permute-start(bf16[32,6272]{1,0:T(8,128)(2,1)S(1)} %shard_map.66), channel_id=1, source_target_pairs={{0,8},{1,25},{2,10},{3,27},{4,12},{5,29},{6,14},{7,31},{8,0},{9,17... | collective-permute-start | bytes 1204232 | tf_op jit(solution)/shard_map/ppermute | solution.py:86
